TPU v7x, 256 devices: a whole 4x4x8 slice. The times are simulated.
256 devices in a mesh: seq: 128 (over y, z, x), head: 2 (over core).
Axes of the slice: x: 4, y: 4, z: 8, core: 2. Of those that a mesh axis runs over, the one named last changes fastest.
Arguments:
- query: bfloat16 [16384, 32, 128], P('seq', 'head'), may hold values from -6 to 6
- key: bfloat16 [16384, 4, 128], P('seq', 'head'), may hold values from -6 to 6
- value: bfloat16 [16384, 4, 128], P('seq', 'head'), may hold values from -6 to 6
- dout: bfloat16 [16384, 32, 128], P('seq', 'head'), may hold values from -0.59765625 to 0.59765625
- saved_out: bfloat16 [16384, 32, 128], P(('seq', 'head')), may hold values from -6 to 6
- saved_lse: float32 [16384, 32], P(('seq', 'head')), may hold values from 3 to 7
- row_token: int32 [16384], P(('seq', 'head')), may hold values from 0 to 16383, as said below
- token_row: int32 [16384], P('seq'), may hold values from 0 to 16383, as said below
- doc_lengths: int32 [128], replicated, may hold values from 1 to 1024, as said below
Outputs:
- dquery: bfloat16 [16384, 32, 128], P('seq', 'head')
- dkey: bfloat16 [16384, 4, 128], P('seq', 'head')
- dvalue: bfloat16 [16384, 4, 128], P('seq', 'head')
Inputs may be any that keep to these rules, and one draw needn't show every extreme that they name: `doc_lengths`: documents sum to 16384 tokens; the first and longest has exactly 1024; every other has at most 256. Every token appears once; token_row is the inverse of row_token. Of the rows of one owner (one index of seq+head), at most 2 belong to the tokens of one index of seq, and some owner reaches 2. `token_row`: the inverse of row_token.
All inputs are finite; a program needn't handle non-finite values.
Results may differ from a plain program's by a relative error of at most 0.0055.
Values may be sent and summed in bfloat16 or wider, within the bound.
A program may use at most 64 MiB of HBM per device.

v0:
```python
import jax
import jax.numpy as jnp
from jax import lax
from jax.sharding import PartitionSpec as P

SPAN = 8


def passed_along(value, axis, steps):
    count = lax.axis_size(axis)
    first, last = (max(0, -steps), min(count, count - steps))
    return lax.ppermute(value, axis, [(source, source + steps) for source in range(first, last)])


def from_behind(block, axis, distance):
    devices = range(lax.axis_size(axis))
    route = [((i - distance) % len(devices), i) for i in devices]
    return lax.ppermute(block, axis, route)


def doc_index(positions, doc_lengths):
    ends = jnp.cumsum(doc_lengths)
    return jnp.sum((ends[None, :] <= positions[:, None]).astype(jnp.int32), axis=1)


def earlier_rank(labels, order):
    same = labels[:, None] == labels[None, :]
    before = order[None, :] < order[:, None]
    return jnp.sum((same & before).astype(jnp.int32), axis=1)


def shards(query, key, value, dout, saved_out, saved_lse, row_token, token_row, doc_lengths):
    f32 = jnp.float32
    bf16 = jnp.bfloat16
    seq_count = lax.axis_size("seq")
    head_count = lax.axis_size("head")
    seq_index = lax.axis_index("seq")
    tok, q_heads, depth = query.shape
    kv_heads = key.shape[1]
    query_groups = q_heads // kv_heads
    own_rows = saved_out.shape[0]
    all_heads = saved_out.shape[1]
    slots = max(2, 4 * own_rows // seq_count)
    scale = depth ** (-0.5)
    target_dev = row_token // tok
    place = target_dev * slots + earlier_rank(target_dev, jnp.arange(own_rows, dtype=jnp.int32))
    out_buf = jnp.zeros((seq_count * slots, all_heads, depth), bf16).at[place].set(saved_out)
    lse_buf = jnp.zeros((seq_count * slots, all_heads), f32).at[place].set(saved_lse)
    got_out = lax.all_to_all(
        lax.all_to_all(
            out_buf.reshape(seq_count, slots, all_heads, depth),
            "seq",
            split_axis=0,
            concat_axis=0,
            tiled=True,
        ),
        "head",
        split_axis=2,
        concat_axis=1,
        tiled=True,
    )
    got_lse = lax.all_to_all(
        lax.all_to_all(
            lse_buf.reshape(seq_count, slots, all_heads),
            "seq",
            split_axis=0,
            concat_axis=0,
            tiled=True,
        ),
        "head",
        split_axis=2,
        concat_axis=1,
        tiled=True,
    )
    source = token_row // own_rows
    pick = source // head_count * (head_count * slots) + source % head_count * slots
    pick = pick + earlier_rank(source, token_row % own_rows)
    out_tok = got_out.reshape(-1, q_heads, depth)[pick]
    token_logsumexp = got_lse.reshape(-1, q_heads)[pick]
    output_dot_gradient = jnp.sum(dout.astype(f32) * out_tok.astype(f32), axis=-1)
    qpos = seq_index * tok + jnp.arange(tok, dtype=jnp.int32)
    qdoc = doc_index(qpos, doc_lengths)
    qgroup = query.reshape(tok, kv_heads, query_groups, depth)
    dgroup = dout.reshape(tok, kv_heads, query_groups, depth)
    lse_t = token_logsumexp.reshape(tok, kv_heads, query_groups).transpose(1, 2, 0)[..., None]
    delta_t = output_dot_gradient.reshape(tok, kv_heads, query_groups).transpose(1, 2, 0)[..., None]

    def grads(kblock, vblock, source_dev):
        kpos = source_dev * tok + jnp.arange(tok, dtype=jnp.int32)
        kdoc = doc_index(kpos, doc_lengths)
        allowed = (kdoc[None, :] == qdoc[:, None]) & (kpos[None, :] <= qpos[:, None])
        scores = jnp.einsum("ihgd,jhd->hgij", qgroup, kblock, preferred_element_type=f32) * scale
        probs = jnp.where(allowed[None, None], jnp.exp(scores - lse_t), 0.0)
        probs_b = probs.astype(bf16)
        dval = jnp.einsum("hgij,ihgd->jhd", probs_b, dgroup, preferred_element_type=f32)
        dprobs = jnp.einsum("ihgd,jhd->hgij", dgroup, vblock, preferred_element_type=f32)
        dscores = (probs * (dprobs - delta_t)).astype(bf16)
        dq = jnp.einsum("hgij,jhd->ihgd", dscores, kblock, preferred_element_type=f32) * scale
        dk = jnp.einsum("hgij,ihgd->jhd", dscores, qgroup, preferred_element_type=f32) * scale
        return (dq, dk, dval)

    def block_terms(kblock, vblock, source_dev):
        return grads(kblock, vblock, source_dev)

    dq_own, dk_own, dv_own = block_terms(key, value, seq_index)

    def turn(step, carry):
        kblock, vblock, dk_acc, dv_acc, dq_acc = carry
        kblock, vblock = passed_along((kblock, vblock), "seq", 1)
        dk_acc, dv_acc = from_behind((dk_acc, dv_acc), "seq", 1)
        source_dev = (seq_index - step) % seq_count
        dq_add, dk_add, dv_add = block_terms(kblock, vblock, source_dev)
        return (kblock, vblock, dk_acc + dk_add, dv_acc + dv_add, dq_acc + dq_add)

    carry = lax.fori_loop(1, SPAN + 1, turn, (key, value, dk_own, dv_own, dq_own))
    dq_total = carry[4]
    dk_total, dv_total = (
        from_behind(carry[2].astype(jnp.bfloat16), "seq", -SPAN).astype(jnp.float32),
        from_behind(carry[3].astype(jnp.bfloat16), "seq", -SPAN).astype(jnp.float32),
    )
    dquery = dq_total.reshape(tok, q_heads, depth).astype(bf16)
    return (dquery, dk_total.astype(bf16), dv_total.astype(bf16))


def solution(mesh):
    placed = (
        P("seq", "head", None),
        P("seq", "head", None),
        P("seq", "head", None),
        P("seq", "head", None),
        P(("seq", "head"), None, None),
        P(("seq", "head"), None),
        P(("seq", "head")),
        P("seq"),
        P(),
    )
    return jax.shard_map(
        shards,
        mesh=mesh,
        in_specs=placed,
        out_specs=(P("seq", "head", None), P("seq", "head", None), P("seq", "head", None)),
        check_vma=False,
    )
```

profile of v0, /device:TPU:8, one launch (start us, length us, event | category | flops | bytes accessed | tf_op | source)
XLA Modules:
  0.0 258.8 jit_solution(9517220062580990088)
XLA Ops:
  4.4 15.4 %all-to-all-start = ((f32[128,2,32]{2,1,0:T(2,128)}), f32[128,2,32]{2,1,0:T(2,128)S(1)}, u32[]{:S(2)}, u32[]{:S(2)}) async-start(f32[128,2,32]{2,1,0:T(2,128)} %bitcast.5), calls=%async_computation | async-start | bytes 262144 | tf_op jit(solution)/shard_map/all_to_all | solution.py:63
  20.1 2.5 scatter_fusion
  22.6 3.7 %copy.132 = bf16[128,2,32,128]{3,1,2,0:T(2,128)(2,1)} copy(bf16[128,2,32,128]{3,2,1,0:T(8,128)(2,1)S(1)} %bitcast.171) | data formatting | bytes 4194304 | tf_op jit(solution)/shard_map/reshape | solution.py:51
  26.3 4.7 %all-to-all-done = f32[128,2,32]{2,1,0:T(2,128)S(1)} async-done(((f32[128,2,32]{2,1,0:T(2,128)}), f32[128,2,32]{2,1,0:T(2,128)S(1)}, u32[]{:S(2)}, u32[]{:S(2)}) %all-to-all-start) | async-done | bytes 32800 | tf_op jit(solution)/shard_map/all_to_all | solution.py:63
  31.1 3.8 %all_to_all.40 = f32[128,2,32]{0,1,2:T(2,128)S(1)} all-to-all(f32[128,2,32]{0,1,2:T(2,128)S(1)} %copy.126), channel_id=1, replica_groups=mesh['seq'=128,'head'=2] {'head'}, dimensions={2} | all-to-all | bytes 65536 | tf_op jit(solution)/shard_map/all_to_all | solution.py:62
  34.8 9.7 %all-to-all-start.2 = ((bf16[128,2,32,128]{3,1,2,0:T(2,128)(2,1)}), bf16[128,2,32,128]{3,1,2,0:T(2,128)(2,1)}, u32[]{:S(2)}, u32[]{:S(2)}) async-start(bf16[128,2,32,128]{3,1,2,0:T(2,128)(2,1)} %copy.132), calls=%async_computation.2 | async-start | bytes 4194304 | tf_op jit(solution)/shard_map/all_to_all | solution.py:50
  48.1 48.3 %all-to-all-done.2 = bf16[128,2,32,128]{3,1,2,0:T(2,128)(2,1)} async-done(((bf16[128,2,32,128]{3,1,2,0:T(2,128)(2,1)}), bf16[128,2,32,128]{3,1,2,0:T(2,128)(2,1)}, u32[]{:S(2)}, u32[]{:S(2)}) %all-to-all-start.2) | async-done | bytes 2097184 | tf_op jit(solution)/shard_map/all_to_all | solution.py:50
  96.3 3.8 %copy.133 = bf16[128,2,32,128]{3,1,0,2:T(2,128)(2,1)S(1)} copy(bf16[128,2,32,128]{3,1,2,0:T(2,128)(2,1)} %all-to-all-done.2) | data formatting | bytes 4194304 | tf_op jit(solution)/shard_map/all_to_all | solution.py:50
  100.1 5.4 %all_to_all.41 = bf16[128,2,32,128]{3,1,0,2:T(2,128)(2,1)S(1)} all-to-all(bf16[128,2,32,128]{3,1,0,2:T(2,128)(2,1)S(1)} %copy.133), channel_id=1, replica_groups=mesh['seq'=128,'head'=2] {'head'}, dimensions={2} | all-to-all | bytes 4194304 | tf_op jit(solution)/shard_map/all_to_all | solution.py:49
  105.5 2.4 copy.134
  108.0 1.8 copy.135
  109.7 2.3 gather_fusion.1
  113.4 137.7 %while.24 = (s32[]{:T(128)}, bf16[128,2,128]{2,0,1:T(8,128)(2,1)S(1)}, bf16[128,2,128]{2,0,1:T(8,128)(2,1)S(1)}, f32[128,2,128]{2,0,1:T(8,128)S(1)}, f32[128,2,1...) while((s32[]{:T(128)}, ...), condition=%wide.region_9.10_spmd.clone, body=%wide.region_7.9_spmd.clone.sunk | while | flops 338100352 | bytes 11523026 | solution.py:115
  113.5 2.5 collective-permute-start
  115.9 2.3 collective-permute-start.1
  118.3 1.9 collective-permute-start.2
  120.2 2.6 collective-permute-start.3
  124.2 2.8 %collective-permute-done.1 = bf16[128,2,128]{2,0,1:T(8,128)(2,1)S(1)} collective-permute-done((bf16[128,2,128]{2,0,1:T(8,128)(2,1)S(1)}, bf16[128,2,128]{2,0,1:T(8,128)(2,1)S(1)}, u32[]{:S(2)}, u32[]{:S(2)}) %collective-permute-start.1) | collective-permute-done | bytes 65568 | tf_op jit(solution)/shard_map/while/body/eval_jaxpr/ppermute | solution.py:12
  127.8 2.1 collective-permute-done.2
  131.9 1.9 collective-permute-start
  133.8 1.9 collective-permute-start.1
  136.4 2.9 %collective-permute-start.3 = (f32[128,2,128]{2,0,1:T(8,128)S(1)}, f32[128,2,128]{2,0,1:T(8,128)S(1)}, u32[]{:S(2)}, u32[]{:S(2)}) collective-permute-start(f32[128,2,128]{2,0,1:T(8,128)S(1)} %get-tuple-element.607), channel_id=1, source_target_pairs={{254,0},{0,2},{2,4},{4,6},{6,8},{8,10},{10,12},{12,14},{14,16},{16... | collective-permute-start | bytes 393224 | tf_op jit(solution)/shard_map/while/body/eval_jaxpr/ppermute | solution.py:18
  139.5 3.4 %collective-permute-done = bf16[128,2,128]{2,0,1:T(8,128)(2,1)S(1)} collective-permute-done((bf16[128,2,128]{2,0,1:T(8,128)(2,1)S(1)}, bf16[128,2,128]{2,0,1:T(8,128)(2,1)S(1)}, u32[]{:S(2)}, u32[]{:S(2)}) %collective-permute-start) | collective-permute-done | bytes 65568 | tf_op jit(solution)/shard_map/while/body/eval_jaxpr/ppermute | solution.py:12
  145.7 2.1 collective-permute-done.2
  149.6 1.9 collective-permute-start
  151.5 1.9 collective-permute-start.1
  155.1 5.5 %collective-permute-done = bf16[128,2,128]{2,0,1:T(8,128)(2,1)S(1)} collective-permute-done((bf16[128,2,128]{2,0,1:T(8,128)(2,1)S(1)}, bf16[128,2,128]{2,0,1:T(8,128)(2,1)S(1)}, u32[]{:S(2)}, u32[]{:S(2)}) %collective-permute-start) | collective-permute-done | bytes 65568 | tf_op jit(solution)/shard_map/while/body/eval_jaxpr/ppermute | solution.py:12
  163.4 1.9 collective-permute-done.2
  167.1 1.9 collective-permute-start
  169.0 1.9 collective-permute-start.1
  171.4 6.6 %collective-permute-done = bf16[128,2,128]{2,0,1:T(8,128)(2,1)S(1)} collective-permute-done((bf16[128,2,128]{2,0,1:T(8,128)(2,1)S(1)}, bf16[128,2,128]{2,0,1:T(8,128)(2,1)S(1)}, u32[]{:S(2)}, u32[]{:S(2)}) %collective-permute-start) | collective-permute-done | bytes 65568 | tf_op jit(solution)/shard_map/while/body/eval_jaxpr/ppermute | solution.py:12
  178.4 1.7 collective-permute-done.1
  180.9 1.7 collective-permute-done.2
  184.3 1.9 collective-permute-start
  186.2 1.9 collective-permute-start.1
  188.7 6.7 %collective-permute-done = bf16[128,2,128]{2,0,1:T(8,128)(2,1)S(1)} collective-permute-done((bf16[128,2,128]{2,0,1:T(8,128)(2,1)S(1)}, bf16[128,2,128]{2,0,1:T(8,128)(2,1)S(1)}, u32[]{:S(2)}, u32[]{:S(2)}) %collective-permute-start) | collective-permute-done | bytes 65568 | tf_op jit(solution)/shard_map/while/body/eval_jaxpr/ppermute | solution.py:12
  195.7 1.7 collective-permute-done.1
  201.3 1.9 collective-permute-start
  203.3 1.9 collective-permute-start.1
  205.7 6.7 %collective-permute-done = bf16[128,2,128]{2,0,1:T(8,128)(2,1)S(1)} collective-permute-done((bf16[128,2,128]{2,0,1:T(8,128)(2,1)S(1)}, bf16[128,2,128]{2,0,1:T(8,128)(2,1)S(1)}, u32[]{:S(2)}, u32[]{:S(2)}) %collective-permute-start) | collective-permute-done | bytes 65568 | tf_op jit(solution)/shard_map/while/body/eval_jaxpr/ppermute | solution.py:12
  212.8 1.6 collective-permute-done.1
  218.2 1.9 collective-permute-start
  220.1 1.9 collective-permute-start.1
  222.5 6.7 %collective-permute-done = bf16[128,2,128]{2,0,1:T(8,128)(2,1)S(1)} collective-permute-done((bf16[128,2,128]{2,0,1:T(8,128)(2,1)S(1)}, bf16[128,2,128]{2,0,1:T(8,128)(2,1)S(1)}, u32[]{:S(2)}, u32[]{:S(2)}) %collective-permute-start) | collective-permute-done | bytes 65568 | tf_op jit(solution)/shard_map/while/body/eval_jaxpr/ppermute | solution.py:12
  234.8 1.9 collective-permute-start
  236.7 1.9 collective-permute-start.1
  239.1 6.8 %collective-permute-done = bf16[128,2,128]{2,0,1:T(8,128)(2,1)S(1)} collective-permute-done((bf16[128,2,128]{2,0,1:T(8,128)(2,1)S(1)}, bf16[128,2,128]{2,0,1:T(8,128)(2,1)S(1)}, u32[]{:S(2)}, u32[]{:S(2)}) %collective-permute-start) | collective-permute-done | bytes 65568 | tf_op jit(solution)/shard_map/while/body/eval_jaxpr/ppermute | solution.py:12
  252.8 3.8 %collective-permute-done.4 = bf16[128,2,128]{2,1,0:T(2,128)(2,1)S(1)} collective-permute-done((bf16[128,2,128]{2,1,0:T(2,128)(2,1)S(1)}, bf16[128,2,128]{2,1,0:T(2,128)(2,1)S(1)}, u32[]{:S(2)}, u32[]{:S(2)}) %collective-permute-start.4) | collective-permute-done | bytes 65568 | tf_op jit(solution)/shard_map/ppermute | solution.py:18
  (173 shorter events, 52.4 us)
Async XLA Ops:
  0.6 19.5 %copy-start.2 = (bf16[64,32,128]{2,1,0:T(8,128)(2,1)S(1)}, bf16[64,32,128]{2,1,0:T(8,128)(2,1)}, u32[]{:S(2)}) copy-start(bf16[64,32,128]{2,1,0:T(8,128)(2,1)} %param.15) | copy-start | bytes 1572868
  4.4 26.6 %all-to-all-start = ((f32[128,2,32]{2,1,0:T(2,128)}), f32[128,2,32]{2,1,0:T(2,128)S(1)}, u32[]{:S(2)}, u32[]{:S(2)}) async-start(f32[128,2,32]{2,1,0:T(2,128)} %bitcast.5), calls=%async_computation | async-start | bytes 262144 | tf_op jit(solution)/shard_map/all_to_all | solution.py:63
  34.8 9.8 %copy-start.6 = (s32[128]{0:T(128)S(1)}, s32[128]{0:T(128)}, u32[]{:S(2)}) copy-start(s32[128]{0:T(128)} %param.19) | copy-start | bytes 1540
  34.8 10.1 %copy-start.3 = (bf16[128,16,128]{2,1,0:T(8,128)(2,1)S(1)}, bf16[128,16,128]{2,1,0:T(8,128)(2,1)}, u32[]{:S(2)}) copy-start(bf16[128,16,128]{2,1,0:T(8,128)(2,1)} %param.11) | copy-start | bytes 1572868
  34.8 10.2 %copy-start = (bf16[128,16,128]{2,1,0:T(8,128)(2,1)S(1)}, bf16[128,16,128]{2,1,0:T(8,128)(2,1)}, u32[]{:S(2)}) copy-start(bf16[128,16,128]{2,1,0:T(8,128)(2,1)} %param.14) | copy-start | bytes 1572868
  34.8 61.5 %all-to-all-start.2 = ((bf16[128,2,32,128]{3,1,2,0:T(2,128)(2,1)}), bf16[128,2,32,128]{3,1,2,0:T(2,128)(2,1)}, u32[]{:S(2)}, u32[]{:S(2)}) async-start(bf16[128,2,32,128]{3,1,2,0:T(2,128)(2,1)} %copy.132), calls=%async_computation.2 | async-start | bytes 4194304 | tf_op jit(solution)/shard_map/all_to_all | solution.py:50
  44.5 0.8 copy-start.1
  44.6 0.9 copy-start.4
  44.6 1.5 copy-start.7
  112.5 1.0 copy-start.5
  113.5 10.4 %collective-permute-start = (bf16[128,2,128]{2,0,1:T(8,128)(2,1)S(1)}, bf16[128,2,128]{2,0,1:T(8,128)(2,1)S(1)}, u32[]{:S(2)}, u32[]{:S(2)}) collective-permute-start(bf16[128,2,128]{2,0,1:T(8,128)(2,1)S(1)} %get-tuple-element.604), channel_id=1, source_target_pairs={{0,2},{2,4},{4,6},{6,8},{8,10},{10,12},{12,14},{14,16},{16,18},{18... | collective-permute-start | bytes 196616 | tf_op jit(solution)/shard_map/while/body/eval_jaxpr/ppermute | solution.py:12
  115.9 11.1 %collective-permute-start.1 = (bf16[128,2,128]{2,0,1:T(8,128)(2,1)S(1)}, bf16[128,2,128]{2,0,1:T(8,128)(2,1)S(1)}, u32[]{:S(2)}, u32[]{:S(2)}) collective-permute-start(bf16[128,2,128]{2,0,1:T(8,128)(2,1)S(1)} %get-tuple-element.605), channel_id=1, source_target_pairs={{0,2},{2,4},{4,6},{6,8},{8,10},{10,12},{12,14},{14,16},{16,18},{18... | collective-permute-start | bytes 196616 | tf_op jit(solution)/shard_map/while/body/eval_jaxpr/ppermute | solution.py:12
  118.3 11.6 %collective-permute-start.2 = (f32[128,2,128]{2,0,1:T(8,128)S(1)}, f32[128,2,128]{2,0,1:T(8,128)S(1)}, u32[]{:S(2)}, u32[]{:S(2)}) collective-permute-start(f32[128,2,128]{2,0,1:T(8,128)S(1)} %get-tuple-element.606), channel_id=1, source_target_pairs={{254,0},{0,2},{2,4},{4,6},{6,8},{8,10},{10,12},{12,14},{14,16},{16... | collective-permute-start | bytes 393224 | tf_op jit(solution)/shard_map/while/body/eval_jaxpr/ppermute | solution.py:18
  120.2 11.4 %collective-permute-start.3 = (f32[128,2,128]{2,0,1:T(8,128)S(1)}, f32[128,2,128]{2,0,1:T(8,128)S(1)}, u32[]{:S(2)}, u32[]{:S(2)}) collective-permute-start(f32[128,2,128]{2,0,1:T(8,128)S(1)} %get-tuple-element.607), channel_id=1, source_target_pairs={{254,0},{0,2},{2,4},{4,6},{6,8},{8,10},{10,12},{12,14},{14,16},{16... | collective-permute-start | bytes 393224 | tf_op jit(solution)/shard_map/while/body/eval_jaxpr/ppermute | solution.py:18
  131.9 11.1 %collective-permute-start = (bf16[128,2,128]{2,0,1:T(8,128)(2,1)S(1)}, bf16[128,2,128]{2,0,1:T(8,128)(2,1)S(1)}, u32[]{:S(2)}, u32[]{:S(2)}) collective-permute-start(bf16[128,2,128]{2,0,1:T(8,128)(2,1)S(1)} %get-tuple-element.604), channel_id=1, source_target_pairs={{0,2},{2,4},{4,6},{6,8},{8,10},{10,12},{12,14},{14,16},{16,18},{18... | collective-permute-start | bytes 196616 | tf_op jit(solution)/shard_map/while/body/eval_jaxpr/ppermute | solution.py:12
  133.8 11.1 %collective-permute-start.1 = (bf16[128,2,128]{2,0,1:T(8,128)(2,1)S(1)}, bf16[128,2,128]{2,0,1:T(8,128)(2,1)S(1)}, u32[]{:S(2)}, u32[]{:S(2)}) collective-permute-start(bf16[128,2,128]{2,0,1:T(8,128)(2,1)S(1)} %get-tuple-element.605), channel_id=1, source_target_pairs={{0,2},{2,4},{4,6},{6,8},{8,10},{10,12},{12,14},{14,16},{16,18},{18... | collective-permute-start | bytes 196616 | tf_op jit(solution)/shard_map/while/body/eval_jaxpr/ppermute | solution.py:12
  135.7 12.0 %collective-permute-start.2 = (f32[128,2,128]{2,0,1:T(8,128)S(1)}, f32[128,2,128]{2,0,1:T(8,128)S(1)}, u32[]{:S(2)}, u32[]{:S(2)}) collective-permute-start(f32[128,2,128]{2,0,1:T(8,128)S(1)} %get-tuple-element.606), channel_id=1, source_target_pairs={{254,0},{0,2},{2,4},{4,6},{6,8},{8,10},{10,12},{12,14},{14,16},{16... | collective-permute-start | bytes 393224 | tf_op jit(solution)/shard_map/while/body/eval_jaxpr/ppermute | solution.py:18
  136.4 12.9 %collective-permute-start.3 = (f32[128,2,128]{2,0,1:T(8,128)S(1)}, f32[128,2,128]{2,0,1:T(8,128)S(1)}, u32[]{:S(2)}, u32[]{:S(2)}) collective-permute-start(f32[128,2,128]{2,0,1:T(8,128)S(1)} %get-tuple-element.607), channel_id=1, source_target_pairs={{254,0},{0,2},{2,4},{4,6},{6,8},{8,10},{10,12},{12,14},{14,16},{16... | collective-permute-start | bytes 393224 | tf_op jit(solution)/shard_map/while/body/eval_jaxpr/ppermute | solution.py:18
  149.6 11.1 %collective-permute-start = (bf16[128,2,128]{2,0,1:T(8,128)(2,1)S(1)}, bf16[128,2,128]{2,0,1:T(8,128)(2,1)S(1)}, u32[]{:S(2)}, u32[]{:S(2)}) collective-permute-start(bf16[128,2,128]{2,0,1:T(8,128)(2,1)S(1)} %get-tuple-element.604), channel_id=1, source_target_pairs={{0,2},{2,4},{4,6},{6,8},{8,10},{10,12},{12,14},{14,16},{16,18},{18... | collective-permute-start | bytes 196616 | tf_op jit(solution)/shard_map/while/body/eval_jaxpr/ppermute | solution.py:12
  151.5 11.1 %collective-permute-start.1 = (bf16[128,2,128]{2,0,1:T(8,128)(2,1)S(1)}, bf16[128,2,128]{2,0,1:T(8,128)(2,1)S(1)}, u32[]{:S(2)}, u32[]{:S(2)}) collective-permute-start(bf16[128,2,128]{2,0,1:T(8,128)(2,1)S(1)} %get-tuple-element.605), channel_id=1, source_target_pairs={{0,2},{2,4},{4,6},{6,8},{8,10},{10,12},{12,14},{14,16},{16,18},{18... | collective-permute-start | bytes 196616 | tf_op jit(solution)/shard_map/while/body/eval_jaxpr/ppermute | solution.py:12
  153.4 11.9 %collective-permute-start.2 = (f32[128,2,128]{2,0,1:T(8,128)S(1)}, f32[128,2,128]{2,0,1:T(8,128)S(1)}, u32[]{:S(2)}, u32[]{:S(2)}) collective-permute-start(f32[128,2,128]{2,0,1:T(8,128)S(1)} %get-tuple-element.606), channel_id=1, source_target_pairs={{254,0},{0,2},{2,4},{4,6},{6,8},{8,10},{10,12},{12,14},{14,16},{16... | collective-permute-start | bytes 393224 | tf_op jit(solution)/shard_map/while/body/eval_jaxpr/ppermute | solution.py:18
  153.5 13.2 %collective-permute-start.3 = (f32[128,2,128]{2,0,1:T(8,128)S(1)}, f32[128,2,128]{2,0,1:T(8,128)S(1)}, u32[]{:S(2)}, u32[]{:S(2)}) collective-permute-start(f32[128,2,128]{2,0,1:T(8,128)S(1)} %get-tuple-element.607), channel_id=1, source_target_pairs={{254,0},{0,2},{2,4},{4,6},{6,8},{8,10},{10,12},{12,14},{14,16},{16... | collective-permute-start | bytes 393224 | tf_op jit(solution)/shard_map/while/body/eval_jaxpr/ppermute | solution.py:18
  167.1 11.0 %collective-permute-start = (bf16[128,2,128]{2,0,1:T(8,128)(2,1)S(1)}, bf16[128,2,128]{2,0,1:T(8,128)(2,1)S(1)}, u32[]{:S(2)}, u32[]{:S(2)}) collective-permute-start(bf16[128,2,128]{2,0,1:T(8,128)(2,1)S(1)} %get-tuple-element.604), channel_id=1, source_target_pairs={{0,2},{2,4},{4,6},{6,8},{8,10},{10,12},{12,14},{14,16},{16,18},{18... | collective-permute-start | bytes 196616 | tf_op jit(solution)/shard_map/while/body/eval_jaxpr/ppermute | solution.py:12
  169.0 11.1 %collective-permute-start.1 = (bf16[128,2,128]{2,0,1:T(8,128)(2,1)S(1)}, bf16[128,2,128]{2,0,1:T(8,128)(2,1)S(1)}, u32[]{:S(2)}, u32[]{:S(2)}) collective-permute-start(bf16[128,2,128]{2,0,1:T(8,128)(2,1)S(1)} %get-tuple-element.605), channel_id=1, source_target_pairs={{0,2},{2,4},{4,6},{6,8},{8,10},{10,12},{12,14},{14,16},{16,18},{18... | collective-permute-start | bytes 196616 | tf_op jit(solution)/shard_map/while/body/eval_jaxpr/ppermute | solution.py:12
  170.9 11.7 %collective-permute-start.2 = (f32[128,2,128]{2,0,1:T(8,128)S(1)}, f32[128,2,128]{2,0,1:T(8,128)S(1)}, u32[]{:S(2)}, u32[]{:S(2)}) collective-permute-start(f32[128,2,128]{2,0,1:T(8,128)S(1)} %get-tuple-element.606), channel_id=1, source_target_pairs={{254,0},{0,2},{2,4},{4,6},{6,8},{8,10},{10,12},{12,14},{14,16},{16... | collective-permute-start | bytes 393224 | tf_op jit(solution)/shard_map/while/body/eval_jaxpr/ppermute | solution.py:18
  171.0 13.0 %collective-permute-start.3 = (f32[128,2,128]{2,0,1:T(8,128)S(1)}, f32[128,2,128]{2,0,1:T(8,128)S(1)}, u32[]{:S(2)}, u32[]{:S(2)}) collective-permute-start(f32[128,2,128]{2,0,1:T(8,128)S(1)} %get-tuple-element.607), channel_id=1, source_target_pairs={{254,0},{0,2},{2,4},{4,6},{6,8},{8,10},{10,12},{12,14},{14,16},{16... | collective-permute-start | bytes 393224 | tf_op jit(solution)/shard_map/while/body/eval_jaxpr/ppermute | solution.py:18
  184.3 11.0 %collective-permute-start = (bf16[128,2,128]{2,0,1:T(8,128)(2,1)S(1)}, bf16[128,2,128]{2,0,1:T(8,128)(2,1)S(1)}, u32[]{:S(2)}, u32[]{:S(2)}) collective-permute-start(bf16[128,2,128]{2,0,1:T(8,128)(2,1)S(1)} %get-tuple-element.604), channel_id=1, source_target_pairs={{0,2},{2,4},{4,6},{6,8},{8,10},{10,12},{12,14},{14,16},{16,18},{18... | collective-permute-start | bytes 196616 | tf_op jit(solution)/shard_map/while/body/eval_jaxpr/ppermute | solution.py:12
  186.2 11.1 %collective-permute-start.1 = (bf16[128,2,128]{2,0,1:T(8,128)(2,1)S(1)}, bf16[128,2,128]{2,0,1:T(8,128)(2,1)S(1)}, u32[]{:S(2)}, u32[]{:S(2)}) collective-permute-start(bf16[128,2,128]{2,0,1:T(8,128)(2,1)S(1)} %get-tuple-element.605), channel_id=1, source_target_pairs={{0,2},{2,4},{4,6},{6,8},{8,10},{10,12},{12,14},{14,16},{16,18},{18... | collective-permute-start | bytes 196616 | tf_op jit(solution)/shard_map/while/body/eval_jaxpr/ppermute | solution.py:12
  188.2 11.5 %collective-permute-start.2 = (f32[128,2,128]{2,0,1:T(8,128)S(1)}, f32[128,2,128]{2,0,1:T(8,128)S(1)}, u32[]{:S(2)}, u32[]{:S(2)}) collective-permute-start(f32[128,2,128]{2,0,1:T(8,128)S(1)} %get-tuple-element.606), channel_id=1, source_target_pairs={{254,0},{0,2},{2,4},{4,6},{6,8},{8,10},{10,12},{12,14},{14,16},{16... | collective-permute-start | bytes 393224 | tf_op jit(solution)/shard_map/while/body/eval_jaxpr/ppermute | solution.py:18
  188.3 12.8 %collective-permute-start.3 = (f32[128,2,128]{2,0,1:T(8,128)S(1)}, f32[128,2,128]{2,0,1:T(8,128)S(1)}, u32[]{:S(2)}, u32[]{:S(2)}) collective-permute-start(f32[128,2,128]{2,0,1:T(8,128)S(1)} %get-tuple-element.607), channel_id=1, source_target_pairs={{254,0},{0,2},{2,4},{4,6},{6,8},{8,10},{10,12},{12,14},{14,16},{16... | collective-permute-start | bytes 393224 | tf_op jit(solution)/shard_map/while/body/eval_jaxpr/ppermute | solution.py:18
  201.3 11.1 %collective-permute-start = (bf16[128,2,128]{2,0,1:T(8,128)(2,1)S(1)}, bf16[128,2,128]{2,0,1:T(8,128)(2,1)S(1)}, u32[]{:S(2)}, u32[]{:S(2)}) collective-permute-start(bf16[128,2,128]{2,0,1:T(8,128)(2,1)S(1)} %get-tuple-element.604), channel_id=1, source_target_pairs={{0,2},{2,4},{4,6},{6,8},{8,10},{10,12},{12,14},{14,16},{16,18},{18... | collective-permute-start | bytes 196616 | tf_op jit(solution)/shard_map/while/body/eval_jaxpr/ppermute | solution.py:12
  203.3 11.1 %collective-permute-start.1 = (bf16[128,2,128]{2,0,1:T(8,128)(2,1)S(1)}, bf16[128,2,128]{2,0,1:T(8,128)(2,1)S(1)}, u32[]{:S(2)}, u32[]{:S(2)}) collective-permute-start(bf16[128,2,128]{2,0,1:T(8,128)(2,1)S(1)} %get-tuple-element.605), channel_id=1, source_target_pairs={{0,2},{2,4},{4,6},{6,8},{8,10},{10,12},{12,14},{14,16},{16,18},{18... | collective-permute-start | bytes 196616 | tf_op jit(solution)/shard_map/while/body/eval_jaxpr/ppermute | solution.py:12
  205.2 11.2 %collective-permute-start.2 = (f32[128,2,128]{2,0,1:T(8,128)S(1)}, f32[128,2,128]{2,0,1:T(8,128)S(1)}, u32[]{:S(2)}, u32[]{:S(2)}) collective-permute-start(f32[128,2,128]{2,0,1:T(8,128)S(1)} %get-tuple-element.606), channel_id=1, source_target_pairs={{254,0},{0,2},{2,4},{4,6},{6,8},{8,10},{10,12},{12,14},{14,16},{16... | collective-permute-start | bytes 393224 | tf_op jit(solution)/shard_map/while/body/eval_jaxpr/ppermute | solution.py:18
  205.3 12.6 %collective-permute-start.3 = (f32[128,2,128]{2,0,1:T(8,128)S(1)}, f32[128,2,128]{2,0,1:T(8,128)S(1)}, u32[]{:S(2)}, u32[]{:S(2)}) collective-permute-start(f32[128,2,128]{2,0,1:T(8,128)S(1)} %get-tuple-element.607), channel_id=1, source_target_pairs={{254,0},{0,2},{2,4},{4,6},{6,8},{8,10},{10,12},{12,14},{14,16},{16... | collective-permute-start | bytes 393224 | tf_op jit(solution)/shard_map/while/body/eval_jaxpr/ppermute | solution.py:18
  218.2 11.1 %collective-permute-start = (bf16[128,2,128]{2,0,1:T(8,128)(2,1)S(1)}, bf16[128,2,128]{2,0,1:T(8,128)(2,1)S(1)}, u32[]{:S(2)}, u32[]{:S(2)}) collective-permute-start(bf16[128,2,128]{2,0,1:T(8,128)(2,1)S(1)} %get-tuple-element.604), channel_id=1, source_target_pairs={{0,2},{2,4},{4,6},{6,8},{8,10},{10,12},{12,14},{14,16},{16,18},{18... | collective-permute-start | bytes 196616 | tf_op jit(solution)/shard_map/while/body/eval_jaxpr/ppermute | solution.py:12
  220.1 11.1 %collective-permute-start.1 = (bf16[128,2,128]{2,0,1:T(8,128)(2,1)S(1)}, bf16[128,2,128]{2,0,1:T(8,128)(2,1)S(1)}, u32[]{:S(2)}, u32[]{:S(2)}) collective-permute-start(bf16[128,2,128]{2,0,1:T(8,128)(2,1)S(1)} %get-tuple-element.605), channel_id=1, source_target_pairs={{0,2},{2,4},{4,6},{6,8},{8,10},{10,12},{12,14},{14,16},{16,18},{18... | collective-permute-start | bytes 196616 | tf_op jit(solution)/shard_map/while/body/eval_jaxpr/ppermute | solution.py:12
  222.0 11.0 %collective-permute-start.2 = (f32[128,2,128]{2,0,1:T(8,128)S(1)}, f32[128,2,128]{2,0,1:T(8,128)S(1)}, u32[]{:S(2)}, u32[]{:S(2)}) collective-permute-start(f32[128,2,128]{2,0,1:T(8,128)S(1)} %get-tuple-element.606), channel_id=1, source_target_pairs={{254,0},{0,2},{2,4},{4,6},{6,8},{8,10},{10,12},{12,14},{14,16},{16... | collective-permute-start | bytes 393224 | tf_op jit(solution)/shard_map/while/body/eval_jaxpr/ppermute | solution.py:18
  222.1 12.3 %collective-permute-start.3 = (f32[128,2,128]{2,0,1:T(8,128)S(1)}, f32[128,2,128]{2,0,1:T(8,128)S(1)}, u32[]{:S(2)}, u32[]{:S(2)}) collective-permute-start(f32[128,2,128]{2,0,1:T(8,128)S(1)} %get-tuple-element.607), channel_id=1, source_target_pairs={{254,0},{0,2},{2,4},{4,6},{6,8},{8,10},{10,12},{12,14},{14,16},{16... | collective-permute-start | bytes 393224 | tf_op jit(solution)/shard_map/while/body/eval_jaxpr/ppermute | solution.py:18
  234.8 11.1 %collective-permute-start = (bf16[128,2,128]{2,0,1:T(8,128)(2,1)S(1)}, bf16[128,2,128]{2,0,1:T(8,128)(2,1)S(1)}, u32[]{:S(2)}, u32[]{:S(2)}) collective-permute-start(bf16[128,2,128]{2,0,1:T(8,128)(2,1)S(1)} %get-tuple-element.604), channel_id=1, source_target_pairs={{0,2},{2,4},{4,6},{6,8},{8,10},{10,12},{12,14},{14,16},{16,18},{18... | collective-permute-start | bytes 196616 | tf_op jit(solution)/shard_map/while/body/eval_jaxpr/ppermute | solution.py:12
  236.7 11.2 %collective-permute-start.1 = (bf16[128,2,128]{2,0,1:T(8,128)(2,1)S(1)}, bf16[128,2,128]{2,0,1:T(8,128)(2,1)S(1)}, u32[]{:S(2)}, u32[]{:S(2)}) collective-permute-start(bf16[128,2,128]{2,0,1:T(8,128)(2,1)S(1)} %get-tuple-element.605), channel_id=1, source_target_pairs={{0,2},{2,4},{4,6},{6,8},{8,10},{10,12},{12,14},{14,16},{16,18},{18... | collective-permute-start | bytes 196616 | tf_op jit(solution)/shard_map/while/body/eval_jaxpr/ppermute | solution.py:12
  238.6 10.8 %collective-permute-start.2 = (f32[128,2,128]{2,0,1:T(8,128)S(1)}, f32[128,2,128]{2,0,1:T(8,128)S(1)}, u32[]{:S(2)}, u32[]{:S(2)}) collective-permute-start(f32[128,2,128]{2,0,1:T(8,128)S(1)} %get-tuple-element.606), channel_id=1, source_target_pairs={{254,0},{0,2},{2,4},{4,6},{6,8},{8,10},{10,12},{12,14},{14,16},{16... | collective-permute-start | bytes 393224 | tf_op jit(solution)/shard_map/while/body/eval_jaxpr/ppermute | solution.py:18
  238.7 12.1 %collective-permute-start.3 = (f32[128,2,128]{2,0,1:T(8,128)S(1)}, f32[128,2,128]{2,0,1:T(8,128)S(1)}, u32[]{:S(2)}, u32[]{:S(2)}) collective-permute-start(f32[128,2,128]{2,0,1:T(8,128)S(1)} %get-tuple-element.607), channel_id=1, source_target_pairs={{254,0},{0,2},{2,4},{4,6},{6,8},{8,10},{10,12},{12,14},{14,16},{16... | collective-permute-start | bytes 393224 | tf_op jit(solution)/shard_map/while/body/eval_jaxpr/ppermute | solution.py:18
  251.2 5.3 %collective-permute-start.4 = (bf16[128,2,128]{2,1,0:T(2,128)(2,1)S(1)}, bf16[128,2,128]{2,1,0:T(2,128)(2,1)S(1)}, u32[]{:S(2)}, u32[]{:S(2)}) collective-permute-start(bf16[128,2,128]{2,1,0:T(2,128)(2,1)S(1)} %copy.171), channel_id=1, source_target_pairs={{16,0},{18,2},{20,4},{22,6},{24,8},{26,10},{28,12},{30,14},{32,16}... | collective-permute-start | bytes 196616 | tf_op jit(solution)/shard_map/ppermute | solution.py:18
  251.4 6.1 %collective-permute-start.5 = (bf16[128,2,128]{2,1,0:T(2,128)(2,1)S(1)}, bf16[128,2,128]{2,1,0:T(2,128)(2,1)S(1)}, u32[]{:S(2)}, u32[]{:S(2)}) collective-permute-start(bf16[128,2,128]{2,1,0:T(2,128)(2,1)S(1)} %copy.170), channel_id=1, source_target_pairs={{16,0},{18,2},{20,4},{22,6},{24,8},{26,10},{28,12},{30,14},{32,16}... | collective-permute-start | bytes 196616 | tf_op jit(solution)/shard_map/ppermute | solution.py:18
where the time goes:
time: 260 us; the launch traced here: 259 us
  waiting for transfers between devices  137 us (53%)
  starting transfers between devices  67.2 us (26%)
  local copies, waits for them, and re-layouts  23.8 us (9%)
  matrix products  14.7 us (6%)
  blocking collectives  9.17 us (4%)
  other arithmetic  5.05 us (2%)
    ppermute x16, waiting for transfers between devices, passed_along(): lax.ppermute(value, axis, [(source, source + steps) for source in range(f...  57.5 us
    all_to_all x1, waiting for transfers between devices, shards(): lax.all_to_all(out_buf.reshape(seq_count, slots, all_heads, depth), 'seq'...  48.3 us
    ppermute x16, starting transfers between devices, passed_along(): lax.ppermute(value, axis, [(source, source + steps) for source in range(f...  31.7 us
    ppermute x18, waiting for transfers between devices, from_behind(): return lax.ppermute(block, axis, route)  26.6 us
    all_to_all x1, starting transfers between devices, shards(): lax.all_to_all(lse_buf.reshape(seq_count, slots, all_heads), 'seq', split...  15.4 us
    ppermute x18, starting transfers between devices, from_behind(): return lax.ppermute(block, axis, route)  10.4 us
    all_to_all x1, starting transfers between devices, shards(): lax.all_to_all(out_buf.reshape(seq_count, slots, all_heads, depth), 'seq'...  9.72 us
    all_to_all x1, blocking collectives, shards(): lax.all_to_all(lax.all_to_all(out_buf.reshape(seq_count, slots, all_heads...  5.42 us
  transfers between devices with their start and end apart: 36, of which 36 were waited for; matrix products, arithmetic and copies ran while one was open for 9% of the time, Pallas kernels for 0%

commit v1 on v0

v1 whole, which is shorter than its diff:
```python
import functools

import jax
import jax.numpy as jnp
from jax import lax
from jax.experimental import pallas as pl
from jax.experimental.pallas import tpu as pltpu
from jax.sharding import PartitionSpec as P

MESH = pl.DeviceIdType.MESH
f32 = jnp.float32
bf16 = jnp.bfloat16
i32 = jnp.int32

TOK = 128
ROWS = 64
CAP = 2
FIRST = 8
REACH = 2
HEADS = 16
GROUPS = 2
QG = 8
D = 128
SCALE = D ** (-0.5)


def kernel(
    n, meta_ref, lse_ref, q_ref, do_ref, k_ref, v_ref, out_ref,
    dq_ref, dk_ref, dv_ref,
    idx_v, idx_s, send, recv, lsend, lrecv, lmat, lse_t, start_row,
    wide, qh, qt, doh, dot_, kr, vr, pbuf, dpbuf, pb, dvs, dvr, dks, dkr, dk0, dqt, delta_t,
    s_idx, s_out, r_out, s_lse, r_lse, s_kv, r_kv, s_dv, r_dv, s_dk, r_dk,
):
    s = lax.axis_index("seq")
    h = lax.axis_index("head")
    me = s * 2 + h
    peers = 2 * n - 1

    barrier = pltpu.get_barrier_semaphore()

    def hello(i, c):
        d = lax.rem(s + i, n)
        for o in range(2):
            pl.semaphore_signal(barrier, inc=1, device_id=(d, o), device_id_type=MESH)
        return c

    lax.fori_loop(1, n, hello, 0)
    pl.semaphore_signal(barrier, inc=1, device_id=(s, 1 - h), device_id_type=MESH)

    sub = lax.broadcasted_iota(i32, (TOK, 128), 0)
    lane = lax.broadcasted_iota(i32, (TOK, 128), 1)
    one = jnp.ones((TOK, 128), i32)
    none = jnp.zeros((TOK, 128), i32)
    tgt_r = jnp.broadcast_to(meta_ref[0:1, :] >> 7, (TOK, 128))
    tgt_c = jnp.transpose(tgt_r)
    same = (tgt_r == tgt_c) & (lane < sub)
    rank_c = jnp.sum(jnp.where(same, one, none), axis=1, keepdims=True)
    slot_c = jnp.where(sub < ROWS, tgt_c * CAP + rank_c, -one)
    for half in range(2):
        hit = slot_c == lane + 128 * half
        row = jnp.sum(jnp.where(hit, sub, none), axis=0, keepdims=True)
        idx_v[half : half + 1, :] = jnp.clip(row, 0, ROWS - 1)
    tr_r = jnp.broadcast_to(meta_ref[1:2, :], (TOK, 128))
    own_r = tr_r >> 6
    tr_c = jnp.transpose(tr_r)
    own_c = jnp.transpose(own_r)
    both = own_r == own_c
    trank_r = jnp.sum(jnp.where(both & (tr_c < tr_r), one, none), axis=0, keepdims=True)
    trank_c = jnp.sum(jnp.where(both & (tr_r < tr_c), one, none), axis=1, keepdims=True)
    idx_v[2:3, :] = jnp.clip(own_r[0:1, :], 0, 2 * n - 1)
    idx_v[3:4, :] = jnp.clip(own_r[0:1, :] * CAP + trank_r, 0, 4 * n - 1)
    idx_v[4:8, :] = jnp.zeros((4, 128), i32)
    to_smem = pltpu.make_async_copy(idx_v, idx_s, s_idx)
    to_smem.start()

    len_r = jnp.broadcast_to(meta_ref[2:3, :], (TOK, 128)).astype(f32)
    ends_c = jnp.sum(jnp.where(lane <= sub, len_r, 0.0), axis=1, keepdims=True)
    pos_r = (lane + s * TOK).astype(f32)
    start_row[...] = jnp.max(jnp.where(ends_c <= pos_r, ends_c, 0.0), axis=0, keepdims=True)

    kr[0] = k_ref[...]
    vr[0] = v_ref[...]
    to_smem.wait()
    pl.semaphore_wait(barrier, peers)

    def feeds(a, jj):
        return (a + jj < n) & ((a + jj < FIRST) | ((a >= FIRST) & (jj <= REACH)))

    def kv_copy(which, jj):
        return pltpu.make_async_remote_copy(
            src_ref=(k_ref, v_ref)[which], dst_ref=(kr, vr)[which].at[jj],
            send_sem=s_kv.at[which, jj], recv_sem=r_kv.at[which, jj],
            device_id=(lax.rem(s + jj, n), h), device_id_type=MESH,
        )

    for jj in range(1, FIRST):
        @pl.when(feeds(s, jj))
        def _():
            kv_copy(0, jj).start()
            kv_copy(1, jj).start()

    def slot_row(k):
        return jnp.clip(idx_s[k // 128, lax.rem(k, 128)], 0, ROWS - 1)

    lane1 = lax.broadcasted_iota(i32, (1, 128), 1)

    def lse_row(d):
        return jnp.where(lane1 < 32, lse_ref[pl.ds(slot_row(2 * d), 1), :], lse_ref[pl.ds(slot_row(2 * d + 1), 1), :])

    def lse_copy(d, o):
        return pltpu.make_async_remote_copy(
            src_ref=lsend.at[d], dst_ref=lrecv.at[me], send_sem=s_lse, recv_sem=r_lse,
            device_id=(d, o), device_id_type=MESH,
        )

    def send_lse(i, c):
        d = lax.rem(s + i, n)
        lsend[d] = lse_row(d)
        lse_copy(d, 0).start()
        lse_copy(d, 1).start()
        return c

    lax.fori_loop(1, n, send_lse, 0)
    own_lse = lse_row(s)
    lsend[s] = own_lse
    lrecv[me] = own_lse
    lse_copy(s, 1 - h).start()

    def out_copy(d, o):
        return pltpu.make_async_remote_copy(
            src_ref=send.at[pl.ds(4 * d + 2 * o, 2)], dst_ref=recv.at[pl.ds(2 * me, 2)],
            send_sem=s_out, recv_sem=r_out, device_id=(d, o), device_id_type=MESH,
        )

    def fill(d):
        for k in range(CAP):
            r = slot_row(2 * d + k)
            for o in range(2):
                send[4 * d + 2 * o + k] = out_ref[r, o * HEADS : (o + 1) * HEADS, :]

    def send_out(i, c):
        d = lax.rem(s + i, n)
        fill(d)
        out_copy(d, 0).start()
        out_copy(d, 1).start()
        return c

    lax.fori_loop(1, n, send_out, 0)
    fill(s)
    out_copy(s, 1 - h).start()
    for k in range(CAP):
        recv[2 * me + k] = send[4 * s + 2 * h + k]

    for src, nat, tra in ((q_ref, qh, qt), (do_ref, doh, dot_)):
        wide[0 : TOK * HEADS] = src[...].astype(f32).reshape(TOK * HEADS, D)
        for hh in range(HEADS):
            x = wide[pl.ds(hh, TOK, stride=HEADS), :]
            g, m = hh // QG, hh % QG
            nat[g, m * TOK : (m + 1) * TOK, :] = x.astype(bf16)
            tra[g, :, m * TOK : (m + 1) * TOK] = jnp.transpose(x).astype(bf16)

    def lse_total():
        return pltpu.make_async_remote_copy(
            src_ref=lsend_all.at[pl.ds(0, peers)], dst_ref=lrecv.at[pl.ds(0, peers)], send_sem=s_lse, recv_sem=r_lse,
            device_id=(s, 1 - h), device_id_type=MESH,
        )

    lsend_all = lrecv
    lse_total().wait_recv()

    def pick_lse(t, c):
        lmat[pl.ds(t, 1), :] = lrecv[jnp.clip(idx_s[2, t], 0, 2 * n - 1)]
        return c

    lax.fori_loop(0, TOK, pick_lse, 0)
    m = lmat[...]
    m = jnp.where(trank_c == 0, m, pltpu.roll(m, 128 - 32, 1))
    m = jnp.where(h == 0, m, pltpu.roll(m, 128 - 16, 1))
    lse_t[...] = jnp.transpose(m)

    blocks = jnp.where(s < FIRST, s + 1, jnp.minimum(s - FIRST, REACH) + 1)

    def back(bufs, bufr, ss, rs, jj):
        return pltpu.make_async_remote_copy(
            src_ref=bufs.at[jj], dst_ref=bufr.at[jj], send_sem=ss.at[jj], recv_sem=rs.at[jj],
            device_id=(lax.rem(s - jj + n, n), h), device_id_type=MESH,
        )

    def ahead(jj, c):
        @pl.when(jj > 0)
        def _():
            kv_copy(0, jj).wait_recv()
            kv_copy(1, jj).wait_recv()

        key_pos = (sub + (s - jj) * TOK).astype(f32)
        allowed = (key_pos <= pos_r) & (key_pos >= start_row[...])
        for g in range(GROUPS):
            k = kr[jj, :, g * D : (g + 1) * D]
            v = vr[jj, :, g * D : (g + 1) * D]
            st = jnp.dot(k, qt[g], preferred_element_type=f32)
            for m in range(QG):
                hh = g * QG + m
                cols = slice(m * TOK, (m + 1) * TOK)
                p = jnp.where(allowed, jnp.exp(st[:, cols] * SCALE - lse_t[hh : hh + 1, :]), 0.0)
                pbuf[jj, g, :, cols] = p
                pb[:, cols] = p.astype(bf16)
            dpbuf[jj, g] = jnp.dot(v, dot_[g], preferred_element_type=f32)
            dvs[jj, :, g * D : (g + 1) * D] = jnp.dot(pb[...], doh[g], preferred_element_type=f32)

        @pl.when(jj > 0)
        def _():
            back(dvs, dvr, s_dv, r_dv, jj).start()

        return c

    lax.fori_loop(0, blocks, ahead, 0)

    dv = dvs[0]
    dk0[...] = dv
    for jj in range(1, FIRST):
        @pl.when(feeds(s, jj))
        def _():
            back(dvs, dvr, s_dv, r_dv, jj).wait_recv()
            dk0[...] += dvr[jj]
    dv_ref[...] = dk0[...].astype(bf16)

    dqt[...] = jnp.zeros_like(dqt)

    out_total = pltpu.make_async_remote_copy(
        src_ref=recv.at[pl.ds(0, 2 * peers)], dst_ref=recv.at[pl.ds(0, 2 * peers)], send_sem=s_out, recv_sem=r_out,
        device_id=(s, 1 - h), device_id_type=MESH,
    )
    out_total.wait_recv()

    def products(t, c):
        x = recv[jnp.clip(idx_s[3, t], 0, 4 * n - 1)].astype(f32) * do_ref[t].astype(f32)
        wide[pl.ds(pl.multiple_of(t * HEADS, HEADS), HEADS), :] = x
        return c

    lax.fori_loop(0, TOK, products, 0)
    acc = jnp.zeros((TOK, 128), f32)
    for hh in range(HEADS):
        x = jnp.sum(wide[pl.ds(hh, TOK, stride=HEADS), :], axis=1, keepdims=True)
        acc = jnp.where(lane == hh, x, acc)
    delta_t[...] = jnp.transpose(acc)

    def after(i, c):
        jj = blocks - 1 - i
        for g in range(GROUPS):
            k = kr[jj, :, g * D : (g + 1) * D]
            for m in range(QG):
                hh = g * QG + m
                cols = slice(m * TOK, (m + 1) * TOK)
                pb[:, cols] = (pbuf[jj, g, :, cols] * (dpbuf[jj, g, :, cols] - delta_t[hh : hh + 1, :])).astype(bf16)
            ds = pb[...]
            dk0[:, g * D : (g + 1) * D] = jnp.dot(ds, qh[g], preferred_element_type=f32) * SCALE
            kt = jnp.transpose(k.astype(f32)).astype(bf16)
            dqt[g] += jnp.dot(kt, ds, preferred_element_type=f32)

        @pl.when(jj > 0)
        def _():
            dks[jj] = dk0[...].astype(bf16)
            back(dks, dkr, s_dk, r_dk, jj).start()

        return c

    lax.fori_loop(0, blocks, after, 0)

    for hh in range(HEADS):
        g, m = hh // QG, hh % QG
        wide[pl.ds(hh, TOK, stride=HEADS), :] = jnp.transpose(dqt[g, :, m * TOK : (m + 1) * TOK]) * SCALE
    dq_ref[...] = wide[0 : TOK * HEADS].reshape(TOK, HEADS, D).astype(bf16)

    for jj in range(1, FIRST):
        @pl.when(feeds(s, jj))
        def _():
            back(dks, dkr, s_dk, r_dk, jj).wait_recv()
            dk0[...] += dkr[jj].astype(f32)
    dk_ref[...] = dk0[...].astype(bf16)

    lse_total().wait_send()
    out_total.wait_send()
    for jj in range(1, FIRST):
        @pl.when(feeds(s, jj))
        def _():
            kv_copy(0, jj).wait_send()
            kv_copy(1, jj).wait_send()

        @pl.when(jj < blocks)
        def _():
            back(dvs, dvr, s_dv, r_dv, jj).wait_send()
            back(dks, dkr, s_dk, r_dk, jj).wait_send()


def shards(query, key, value, dout, saved_out, saved_lse, row_token, token_row, doc_lengths):
    n = lax.axis_size("seq")
    meta = jnp.stack([jnp.pad(row_token, (0, TOK - ROWS), constant_values=-1), token_row, doc_lengths])
    lse4 = jnp.concatenate([saved_lse] * 4, axis=1)
    k2 = key.reshape(TOK, GROUPS * D)
    v2 = value.reshape(TOK, GROUPS * D)
    vm = pl.BlockSpec(memory_space=pltpu.VMEM)
    dma = pltpu.SemaphoreType.DMA
    dq, dk, dv = pl.pallas_call(
        functools.partial(kernel, n),
        out_shape=(
            jax.ShapeDtypeStruct((TOK, HEADS, D), bf16),
            jax.ShapeDtypeStruct((TOK, GROUPS * D), bf16),
            jax.ShapeDtypeStruct((TOK, GROUPS * D), bf16),
        ),
        in_specs=[vm] * 7,
        out_specs=(vm, vm, vm),
        scratch_shapes=[
            pltpu.VMEM((8, 128), i32),
            pltpu.SMEM((8, 128), i32),
            pltpu.VMEM((4 * n, HEADS, D), bf16),
            pltpu.VMEM((4 * n, HEADS, D), bf16),
            pltpu.VMEM((n, 1, 128), f32),
            pltpu.VMEM((2 * n, 1, 128), f32),
            pltpu.VMEM((TOK, 128), f32),
            pltpu.VMEM((128, TOK), f32),
            pltpu.VMEM((1, 128), f32),
            pltpu.VMEM((TOK * HEADS + HEADS, D), f32),
            pltpu.VMEM((GROUPS, QG * TOK, D), bf16),
            pltpu.VMEM((GROUPS, D, QG * TOK), bf16),
            pltpu.VMEM((GROUPS, QG * TOK, D), bf16),
            pltpu.VMEM((GROUPS, D, QG * TOK), bf16),
            pltpu.VMEM((FIRST, TOK, GROUPS * D), bf16),
            pltpu.VMEM((FIRST, TOK, GROUPS * D), bf16),
            pltpu.VMEM((FIRST, GROUPS, TOK, QG * TOK), f32),
            pltpu.VMEM((FIRST, GROUPS, TOK, QG * TOK), f32),
            pltpu.VMEM((TOK, QG * TOK), bf16),
            pltpu.VMEM((FIRST, TOK, GROUPS * D), f32),
            pltpu.VMEM((FIRST, TOK, GROUPS * D), f32),
            pltpu.VMEM((FIRST, TOK, GROUPS * D), bf16),
            pltpu.VMEM((FIRST, TOK, GROUPS * D), bf16),
            pltpu.VMEM((TOK, GROUPS * D), f32),
            pltpu.VMEM((GROUPS, D, QG * TOK), f32),
            pltpu.VMEM((128, TOK), f32),
            dma, dma, dma, dma, dma,
            dma((2, FIRST)), dma((2, FIRST)),
            dma((FIRST,)), dma((FIRST,)), dma((FIRST,)), dma((FIRST,)),
        ],
        compiler_params=pltpu.CompilerParams(
            collective_id=0, has_side_effects=True, vmem_limit_bytes=58 * 1024 * 1024
        ),
        name="grads",
    )(meta, lse4, query, dout, k2, v2, saved_out)
    return dq, dk.reshape(TOK, GROUPS, D), dv.reshape(TOK, GROUPS, D)


def solution(mesh):
    placed = (
        P("seq", "head", None),
        P("seq", "head", None),
        P("seq", "head", None),
        P("seq", "head", None),
        P(("seq", "head"), None, None),
        P(("seq", "head"), None),
        P(("seq", "head")),
        P("seq"),
        P(),
    )
    return jax.shard_map(
        shards,
        mesh=mesh,
        in_specs=placed,
        out_specs=(P("seq", "head", None), P("seq", "head", None), P("seq", "head", None)),
        check_vma=False,
    )
```

time: 260 us -> 100 us (0.38)
  the two profiles are of different devices: /device:TPU:8 before, /device:TPU:1 now
where the time goes in v1:
time: 100 us; the launch traced here: 99.9 us
  Pallas kernels  90.2 us (90%)
  local copies, waits for them, and re-layouts  7.04 us (7%)
  other arithmetic  1.97 us (2%)
    pallas_call x1, Pallas kernels, shards(): pl.pallas_call(functools.partial(kernel, n), out_shape=(jax.ShapeDtypeStr...  90.2 us
    unnamed x6, local copies, waits for them, and re-layouts  2.67 us
    reshape x2, local copies, waits for them, and re-layouts, shards(): return (dq, dk.reshape(TOK, GROUPS, D), dv.reshape(TOK, GROUPS, D))  2.17 us

profile of v1, /device:TPU:1, one launch (start us, length us, event | category | flops | bytes accessed | tf_op | source)
XLA Modules:
  0.0 99.9 jit_solution(13687685810550970394)
XLA Ops:
  0.6 0.0 copy-start.1
  0.6 0.7 pad_bitcast_fusion
  1.3 1.3 %pad_add_fusion.meta_ref = s32[3,128]{1,0:T(4,128)} fusion(s32[1,128]{1,0:T(1,128)} %bitcast.12, s32[1,128]{1,0:T(1,128)} %bitcast.13, s32[1,128]{1,0:T(1,128)S(1)} %pad_bitcast_fusion), kind=kLoop, calls=%fused_computation.3 | loop fusion | flops 768 | bytes 3072 | tf_op jit(solution)/shard_map/stack | solution.py:297
  2.6 0.8 copy.12
  3.4 0.7 pad_maximum_fusion.lse_ref
  4.1 0.0 copy-done.1
  4.1 1.5 %copy_bitcast_fusion = (bf16[128,256]{1,0:T(8,128)(2,1)}, bf16[128,256]{1,0:T(8,128)(2,1)}) fusion(bf16[16,8,2,128]{3,2,1,0:T(2,128)(2,1)S(1)} %bitcast.10, bf16[16,8,2,128]{3,2,1,0:T(2,128)(2,1)} %bitcast.11), kind=kLoop, calls=%fused_computation | loop fusion | bytes 262144 | tf_op jit(solution)/shard_map/reshape | solution.py:300
  5.6 90.2 %grads.1 = (bf16[128,16,128]{2,1,0:T(8,128)(2,1)}, bf16[128,256]{1,0:T(8,128)(2,1)}, bf16[128,256]{1,0:T(8,128)(2,1)}) custom-call(s32[3,128]{1,0:T(4,128)} %pad_add_fusion.meta_ref, f32[64,128]{1,0:T(8,128)} %pad_maximum_fusion.lse_ref, bf16[128,16,128]{2,1,0:T(8,128)(2,1)} %q_ref.1, bf16[128,16,128]{2,1,0:T(8,128)(2,1)} %do_ref.1, ...), custom_call_target="tpu_custom_call" | custom-call | tf_op jit(solution)/shard_map/grads/pallas_call | solution.py:303
  95.8 0.0 copy-start
  95.8 1.5 %reshape.20 = bf16[128,2,128]{2,1,0:T(2,128)(2,1)} reshape(bf16[128,256]{1,0:T(8,128)(2,1)} %get-tuple-element.7) | data formatting | bytes 131072 | tf_op jit(solution)/shard_map/reshape | solution.py:348
  97.4 0.0 copy-done
  97.4 0.6 reshape.21
  98.0 1.9 %copy.21 = bf16[128,16,128]{2,1,0:T(8,128)(2,1)} copy(bf16[128,16,128]{2,1,0:T(8,128)(2,1)} %get-tuple-element.14) | data formatting | bytes 1048576
Async XLA Ops:
  0.6 3.5 %copy-start.1 = (bf16[128,2,128]{2,1,0:T(2,128)(2,1)S(1)}, bf16[128,2,128]{2,1,0:T(2,128)(2,1)}, u32[]{:S(2)}) copy-start(bf16[128,2,128]{2,1,0:T(2,128)(2,1)} %param.11) | copy-start | bytes 196612
  95.8 1.5 %copy-start = (bf16[128,256]{1,0:T(8,128)(2,1)S(1)}, bf16[128,256]{1,0:T(8,128)(2,1)}, u32[]{:S(2)}) copy-start(bf16[128,256]{1,0:T(8,128)(2,1)} %get-tuple-element.8) | copy-start | bytes 196612
